TPU v7x, 32 devices: a whole 2x2x4 slice. The times are simulated.
32 devices in a mesh: groups: 2 (over x), dp: 2 (over core), feat: 8 (over z, y).
Axes of the slice: x: 2, y: 2, z: 4, core: 2. Of those that a mesh axis runs over, the one named last changes fastest.
Arguments:
- tokens: bfloat16 [8192, 16384], P(('groups', 'dp'), 'feat'), parts along dimension 0, may hold values from -6 to 6
- block_weights: bfloat16 [24, 2048, 13312], P('feat'), may hold values from -0.078125 to 0.078125
- low_in: bfloat16 [16384, 256], P('feat'), may hold values from -0.046875 to 0.046875
- low_out: bfloat16 [256, 106496], P(None, 'feat'), may hold values from -0.375 to 0.375
Outputs:
- hidden: bfloat16 [8192, 53248], P(('groups', 'dp'), 'feat'), parts along dimension 0
There are 2 independent parts, one for each index of `groups`. A program takes and returns all parts, laid end to end along the dimension named above; an argument that names none is the same for every part. Nothing has to cross between parts.
All inputs are finite; a program needn't handle non-finite values.
Results may differ from a plain program's by a relative error of at most 0.005.
Values may be sent and summed in bfloat16 or wider, within the bound.
No kernel may reach another device: no remote copies, remote signals or barrier semaphores. Data moves between devices by JAX's collectives and lax.ppermute only.
A program may use at most 704 MiB of HBM per device.

v0:
```python
import jax
import jax.numpy as jnp
from jax import lax
from jax.sharding import PartitionSpec as P

BIT_A = 0
BIT_B = 2


def from_partner(array, axis, apart):
    return lax.ppermute(array, axis, [(i, i ^ 1 << apart) for i in range(lax.axis_size(axis))])


def shards(tokens, block_weights, low_in, low_out):
    half_width = block_weights.shape[2] // 2
    near_part = from_partner(tokens, "feat", BIT_A)
    far_part = from_partner(tokens, "feat", BIT_B)
    partial_latent = jnp.dot(tokens, low_in, preferred_element_type=jnp.float32)
    latent = lax.psum(partial_latent, "feat").astype(jnp.bfloat16)
    low_part = jnp.dot(latent, low_out, preferred_element_type=jnp.float32)
    combined = low_part + jnp.dot(tokens, block_weights[0], preferred_element_type=jnp.float32)
    combined = combined + jnp.dot(near_part, block_weights[1], preferred_element_type=jnp.float32)
    combined = combined + jnp.dot(far_part, block_weights[2], preferred_element_type=jnp.float32)
    gate_part = combined[:, :half_width]
    up_part = combined[:, half_width:]
    return (jax.nn.silu(gate_part) * up_part).astype(jnp.bfloat16)


def solution(mesh):
    in_specs = (
        P(("groups", "dp"), "feat"),
        P("feat", None, None),
        P("feat", None),
        P(None, "feat"),
    )
    out_specs = P(("groups", "dp"), "feat")
    return jax.shard_map(shards, mesh=mesh, in_specs=in_specs, out_specs=out_specs, check_vma=False)
```

profile of v0, /device:TPU:0, one launch (start us, length us, event | category | flops | bytes accessed | tf_op | source)
XLA Modules:
  0.0 834.5 jit_solution(14690890070012440934)
XLA Ops:
  0.0 0.0 copy-start
  0.0 4.0 collective-permute-start.1
  4.0 1.5 collective-permute-start
  5.6 0.0 copy-start.1
  5.6 125.1 %fusion.5 = f32[2048,13312]{1,0:T(8,128)} fusion(bf16[2048,2048]{1,0:T(8,128)(2,1)} %param.4, bf16[3,2048,13312]{2,1,0:T(8,128)(2,1)} %param.5), kind=kOutput, calls=%fused_computation.7 | convolution fusion | flops 111669149696 | bytes 171966464 | tf_op jit(solution)/shard_map/dot_general | solution.py:21
  130.7 0.0 copy-done
  130.7 0.0 copy-done.1
  130.7 3.8 fusion.14
  134.4 312.1 %all-reduce.1 = bf16[2048,256]{1,0:T(8,128)(2,1)S(1)} all-reduce(f32[2048,256]{1,0:T(8,128)} %fusion.14), channel_id=1, replica_groups=mesh['groups'=2,'dp'=2,'feat'=8] {'feat'}, use_global_device_ids=true, to_apply=%region_0.0 | all-reduce | flops 524288 | bytes 3145728 | tf_op jit(solution)/shard_map/psum | solution.py:19
  446.5 39.5 %fusion.15 = f32[2048,13312]{1,0:T(8,128)} fusion(bf16[2048,256]{1,0:T(8,128)(2,1)S(1)} %all-reduce.1, bf16[256,13312]{1,0:T(8,128)(2,1)} %param.7), kind=kOutput, calls=%fused_computation.15 | convolution fusion | flops 13958643712 | bytes 116916224 | tf_op jit(solution)/shard_map/dot_general | solution.py:20
  486.0 0.0 collective-permute-done
  486.0 123.8 %fusion.3 = f32[2048,13312]{1,0:T(8,128)} fusion(bf16[2048,2048]{1,0:T(8,128)(2,1)} %collective-permute-done, bf16[3,2048,13312]{2,1,0:T(8,128)(2,1)} %param.5), kind=kOutput, calls=%fused_computation.5 | convolution fusion | flops 111669149696 | bytes 171966464 | tf_op jit(solution)/shard_map/dot_general | solution.py:22
  609.7 0.0 collective-permute-done.1
  609.7 180.2 %add_add_fusion = f32[2048,13312]{1,0:T(8,128)} fusion(f32[2048,13312]{1,0:T(8,128)} %fusion.3, f32[2048,13312]{1,0:T(8,128)} %fusion.15, f32[2048,13312]{1,0:T(8,128)} %fusion.5, bf16[2048,2048]{1,0:T(8,128)(2,1)} %collective-permute-done.1, bf16[3,2048,13312]{2,1,0:T(8,128)(2,1)} %param.5), kind=kOutput, calls=%fused_computation | convolution fusion | flops 111750938624 | bytes 499122176 | tf_op jit(solution)/shard_map/dot_general | solution.py:23
  789.9 44.5 %fusion = bf16[2048,6656]{1,0:T(8,128)(2,1)} fusion(f32[2048,13312]{1,0:T(8,128)} %add_add_fusion), kind=kLoop, calls=%fused_computation.2 | loop fusion | flops 81788928 | bytes 136314880 | tf_op jit(solution)/shard_map/convert_element_type | solution.py:26
Async XLA Ops:
  0.0 130.7 %copy-start = (bf16[2048,256]{1,0:T(8,128)(2,1)S(1)}, bf16[2048,256]{1,0:T(8,128)(2,1)}, u32[]{:S(2)}) copy-start(bf16[2048,256]{1,0:T(8,128)(2,1)} %param.6) | copy-start | bytes 3145732
  0.0 609.7 %collective-permute-start.1 = (bf16[2048,2048]{1,0:T(8,128)(2,1)}, bf16[2048,2048]{1,0:T(8,128)(2,1)}, u32[]{:S(2)}, u32[]{:S(2)}) collective-permute-start(bf16[2048,2048]{1,0:T(8,128)(2,1)} %param.4), channel_id=1, source_target_pairs={{0,4},{1,5},{2,6},{3,7},{4,0},{5,1},{6,2},{7,3},{8,12},{9,13},{10,... | collective-permute-start | bytes 25165832 | tf_op jit(solution)/shard_map/ppermute | solution.py:11
  4.0 481.9 %collective-permute-start = (bf16[2048,2048]{1,0:T(8,128)(2,1)}, bf16[2048,2048]{1,0:T(8,128)(2,1)}, u32[]{:S(2)}, u32[]{:S(2)}) collective-permute-start(bf16[2048,2048]{1,0:T(8,128)(2,1)} %param.4), channel_id=1, source_target_pairs={{0,1},{1,0},{2,3},{3,2},{4,5},{5,4},{6,7},{7,6},{8,9},{9,8},{10,11... | collective-permute-start | bytes 25165832 | tf_op jit(solution)/shard_map/ppermute | solution.py:11
  5.6 125.1 %copy-start.1 = (bf16[2048,2048]{1,0:T(8,128)(2,1)S(1)}, bf16[2048,2048]{1,0:T(8,128)(2,1)}, u32[]{:S(2)}) copy-start(bf16[2048,2048]{1,0:T(8,128)(2,1)} %param.4) | copy-start | bytes 25165828
where the time goes:
time: 835 us; the launch traced here: 834 us
  matrix products  472 us (57%)
  blocking collectives  312 us (37%)
  other arithmetic  44.5 us (5%)
    psum x1, blocking collectives, shards(): latent = lax.psum(partial_latent, 'feat').astype(jnp.bfloat16)  312 us
    dot_general x1, matrix products, shards(): jnp.dot(far_part, block_weights[2], preferred_element_type=jnp.float32)  180 us
    dot_general x1, matrix products, shards(): jnp.dot(tokens, block_weights[0], preferred_element_type=jnp.float32)  125 us
    dot_general x1, matrix products, shards(): jnp.dot(near_part, block_weights[1], preferred_element_type=jnp.float32)  124 us
    convert_element_type x1, other arithmetic, shards(): return (jax.nn.silu(gate_part) * up_part).astype(jnp.bfloat16)  44.5 us
    dot_general x1, matrix products, shards(): low_part = jnp.dot(latent, low_out, preferred_element_type=jnp.float32)  39.5 us
  transfers between devices with their start and end apart: 2, of which 0 were waited for; matrix products, arithmetic and copies ran while one was open for 35% of the time, Pallas kernels for 0%

commit v1 on v0

--- a/solution.py
+++ b/solution.py
@@ -1,17 +1,23 @@
+import functools
+
 import jax
 import jax.numpy as jnp
 from jax import lax
+from jax.experimental import pallas as pl
+from jax.experimental.pallas import tpu as pltpu
 from jax.sharding import PartitionSpec as P
 
 BIT_A = 0
 BIT_B = 2
+VMEM_LIMIT = 56 * 1024 * 1024
+FIRST_ROWS, HEAD_ROWS, SECOND_ROWS = 9, 2, 5
 
 
 def from_partner(array, axis, apart):
     return lax.ppermute(array, axis, [(i, i ^ 1 << apart) for i in range(lax.axis_size(axis))])
 
 
-def shards(tokens, block_weights, low_in, low_out):
+def plain(tokens, block_weights, low_in, low_out):
     half_width = block_weights.shape[2] // 2
     near_part = from_partner(tokens, "feat", BIT_A)
     far_part = from_partner(tokens, "feat", BIT_B)
@@ -26,6 +32,174 @@
     return (jax.nn.silu(gate_part) * up_part).astype(jnp.bfloat16)
 
 
+def row_cuts(rows, most):
+    parts = -(-rows // most)
+    while rows % parts or rows // parts % 16:
+        parts += 1
+    return [(k * (rows // parts), rows // parts) for k in range(parts)]
+
+
+def product_kernel(plan, *refs):
+    tile, pieces, terms, low, add, gated, sends = plan
+    refs = list(refs)
+    take = lambda count: [refs.pop(0) for _ in range(count)]
+    factors = [(take(len(pieces)), take(2)) for _ in range(terms)]
+    if low:
+        factors.append((take(1), take(2)))
+    total_ref = take(1)[0] if add else None
+    sent_sem = refs.pop() if sends else None
+    sent_refs = refs[len(refs) - len(sends):]
+    out_ref = refs[len(refs) - len(sends) - 1]
+    copies = [
+        pltpu.make_async_copy(factors[0][0][0].at[pl.ds(first, size), :], sent_refs[k], sent_sem.at[k])
+        for k, (first, size) in enumerate(sends)
+    ]
+    if copies:
+        @pl.when(pl.program_id(0) == 0)
+        def _():
+            for copy in copies:
+                copy.start()
+
+    cuts = []
+    for k, rows in enumerate(pieces):
+        cuts += [(k, sum(pieces[:k]), first, size) for first, size in row_cuts(rows, 288 if gated else 512)]
+    for piece, before, first, size in cuts:
+        here = pl.ds(before + first, size)
+        halves = []
+        for k in range(2):
+            value = None
+            for x_refs, weight_refs in factors:
+                x = x_refs[0][here, :] if len(x_refs) == 1 else x_refs[piece][pl.ds(first, size), :]
+                term = jnp.dot(x, weight_refs[k][...], preferred_element_type=jnp.float32)
+                value = term if value is None else value + term
+            if add:
+                value = value + total_ref[here, k * tile:(k + 1) * tile]
+            halves.append(value)
+        if gated:
+            gate, up = halves
+            out_ref[here, :] = (gate / (1.0 + jnp.exp(-gate)) * up).astype(out_ref.dtype)
+        else:
+            for k in range(2):
+                out_ref[here, k * tile:(k + 1) * tile] = halves[k]
+    if copies:
+        @pl.when(pl.program_id(0) == pl.num_programs(0) - 1)
+        def _():
+            for copy in copies:
+                copy.wait()
+
+
+def product(tile, factors, weights, low=None, total=None, total_at=0, hidden=None, sends=None, cheaper=1):
+    pieces = tuple(piece.shape[0] for piece in factors[0][0])
+    rows, depth = sum(pieces), weights.shape[1]
+    width = weights.shape[2]
+    tiles = width // 2 // tile
+    once = pl.Buffered(1)
+    operands, in_specs = [], []
+    for x, slot in factors:
+        operands += [*x, weights, weights]
+        in_specs += [pl.BlockSpec(piece.shape, lambda j: (0, 0), pipeline_mode=once) for piece in x]
+        in_specs += [
+            pl.BlockSpec((None, depth, tile), lambda j, slot=slot: (slot, 0, j)),
+            pl.BlockSpec((None, depth, tile), lambda j, slot=slot: (slot, 0, j + tiles)),
+        ]
+    span = depth * len(factors)
+    if low is not None:
+        latent, latent_at, low_out = low
+        rank = low_out.shape[0]
+        operands += [latent, low_out, low_out]
+        in_specs += [
+            pl.BlockSpec((pl.Element(rows), pl.Element(rank)), lambda j: (latent_at, 0), pipeline_mode=once),
+            pl.BlockSpec((rank, tile), lambda j: (0, j)),
+            pl.BlockSpec((rank, tile), lambda j: (0, j + tiles)),
+        ]
+        span += rank
+    moved = (rows + width) * span * 2
+    aliases = {}
+    if total is not None:
+        if hidden is None:
+            aliases = {len(operands): 0}
+        operands.append(total)
+        in_specs.append(pl.BlockSpec((pl.Element(rows), pl.Element(2 * tile)), lambda j: (total_at, j * 2 * tile)))
+        moved += rows * width * 4
+    if hidden is not None:
+        all_rows, first, so_far = hidden
+        if so_far is not None:
+            aliases = {len(operands): 0}
+            operands.append(so_far)
+            in_specs.append(pl.BlockSpec(memory_space=pl.ANY))
+        out_shape = [jax.ShapeDtypeStruct((all_rows, width // 2), jnp.bfloat16)]
+        out_specs = [pl.BlockSpec((pl.Element(rows), pl.Element(tile)), lambda j: (first, j * tile))]
+        moved += rows * width
+    else:
+        out_shape = [jax.ShapeDtypeStruct((rows if total is None else total.shape[0], width), jnp.float32)]
+        out_specs = [pl.BlockSpec((pl.Element(rows), pl.Element(2 * tile)), lambda j: (total_at, j * 2 * tile))]
+        moved += rows * width * 4
+    scratch = []
+    for _, size in sends or ():
+        out_shape.append(jax.ShapeDtypeStruct((size, depth), weights.dtype))
+        out_specs.append(pl.BlockSpec(memory_space=pl.ANY))
+        scratch = [pltpu.SemaphoreType.DMA((len(sends),))]
+    plan = (tile, pieces, len(factors), low is not None, total is not None, hidden is not None, sends or ())
+    found = pl.pallas_call(
+        functools.partial(product_kernel, plan),
+        grid=(tiles,),
+        in_specs=in_specs,
+        out_specs=out_specs,
+        out_shape=out_shape,
+        scratch_shapes=scratch,
+        input_output_aliases=aliases,
+        compiler_params=pltpu.CompilerParams(vmem_limit_bytes=VMEM_LIMIT),
+        cost_estimate=pl.CostEstimate(
+            flops=2 * rows * span * width // cheaper, bytes_accessed=moved // cheaper, transcendentals=0 if hidden is None else rows * width // 2
+        ),
+    )(*operands)
+    return found if sends else found[0]
+
+
+def after(value, earlier):
+    return lax.optimization_barrier((value, earlier))
+
+
+def shards(tile, tokens, block_weights, low_in, low_out):
+    rows = tokens.shape[0]
+    count = lax.axis_size("feat")
+    cut = rows * FIRST_ROWS // 16
+    head, mid = rows * HEAD_ROWS // 16, rows * SECOND_ROWS // 16
+    mix = functools.partial(product, tile, weights=block_weights)
+
+    early_rows = lax.slice_in_dim(tokens, 0, cut)
+    near_early = from_partner(early_rows, "feat", BIT_A)
+    late_rows, _ = after(lax.slice_in_dim(tokens, cut, rows), early_rows)
+    far_late = from_partner(late_rows, "feat", BIT_B)
+    tokens, late_rows = after(tokens, late_rows)
+    far_head = from_partner(lax.slice_in_dim(tokens, 0, head), "feat", BIT_B)
+    partial = jnp.dot(tokens, low_in, preferred_element_type=jnp.float32)
+    late_rows, partial = after(late_rows, partial)
+    near_late = from_partner(late_rows, "feat", BIT_A)
+
+    sides = [[i for i in range(count) if (i >> BIT_B & 1) == side] for side in range(2)]
+    latent = lax.psum_scatter(partial, "feat", scatter_dimension=0, axis_index_groups=sides, tiled=True)
+
+    total, held_a, held_b = mix([([tokens], 0)], sends=[(head, mid - head), (mid, cut - mid)])
+    (latent, near_early), total = after((latent, near_early), total)
+    across = from_partner(latent.astype(jnp.bfloat16), "feat", BIT_B)
+
+    total = mix([([near_early], 1)], total=total, cheaper=16)
+    (across, near_late, far_head, held_a, held_b), total = after((across, near_late, far_head, held_a, held_b), total)
+    latent = (latent + across.astype(jnp.float32)).astype(jnp.bfloat16)
+    held_a, latent = after(held_a, latent)
+    far_a = from_partner(held_a, "feat", BIT_B)
+    latent = lax.all_gather(latent, "feat", axis=0, axis_index_groups=sides, tiled=True)
+
+    total = mix([([near_late], 1)], total=total, total_at=cut, cheaper=16)
+    (latent, held_b), total = after((latent, held_b), total)
+    far_b = from_partner(held_b, "feat", BIT_B)
+
+    hidden = mix([([far_late], 2)], low=(latent, cut, low_out), total=total, total_at=cut, hidden=(rows, cut, None), cheaper=16)
+    hidden = mix([([far_head, far_a], 2)], low=(latent, 0, low_out), total=total, hidden=(rows, 0, hidden))
+    return mix([([far_b], 2)], low=(latent, mid, low_out), total=total, total_at=mid, hidden=(rows, mid, hidden))
+
+
 def solution(mesh):
     in_specs = (
         P(("groups", "dp"), "feat"),
@@ -34,4 +208,17 @@
         P(None, "feat"),
     )
     out_specs = P(("groups", "dp"), "feat")
-    return jax.shard_map(shards, mesh=mesh, in_specs=in_specs, out_specs=out_specs, check_vma=False)
+
+    def hidden(tokens, block_weights, low_in, low_out):
+        count = mesh.shape["feat"]
+        rows = tokens.shape[0] // (mesh.shape["groups"] * mesh.shape["dp"])
+        half_width = block_weights.shape[2] // 2
+        tile = next((t for t in (512, 256, 128) if half_width % t == 0), 0)
+        fits = tile and rows % 256 == 0 and rows <= 2048 and block_weights.shape[1] <= 2048 and block_weights.shape[1] % 128 == 0
+        fits = fits and count & (count - 1) == 0 and count > 1 << BIT_B and rows % count == 0 and BIT_A < BIT_B and low_in.shape[1] % 128 == 0
+        body = functools.partial(shards, tile) if fits else plain
+        return jax.shard_map(body, mesh=mesh, in_specs=in_specs, out_specs=out_specs, check_vma=False)(
+            tokens, block_weights, low_in, low_out
+        )
+
+    return hidden

time: 835 us -> 466 us (0.56)
  matrix products: 472 us -> 3.74 us
  Pallas kernels: 0 us -> 419 us
  blocking collectives: 312 us -> 0 us
  other arithmetic: 44.5 us -> 3.48 us
  between operations: 0.02 us -> 13.4 us
  local copies, waits for them, and re-layouts: 0.01 us -> 9.97 us
    dot_general x5 -> x1, matrix products: 472 us -> 3.74 us  [shards(): partial = jnp.dot(tokens, low_in, preferred_element_type=jnp.float32)]
    pallas_call x0 -> x6, Pallas kernels: none -> 419 us  [product(): pl.pallas_call(functools.partial(product_kernel, plan), grid=(tiles,), in...]
    psum x1 -> x0, blocking collectives: 312 us -> none  [shards(): latent = lax.psum(partial_latent, 'feat').astype(jnp.bfloat16)]
    convert_element_type x1 -> x2, other arithmetic: 44.5 us -> 3.48 us  [the longest x1 1.77 us: shards(): across = from_partner(latent.astype(jnp.bfloat16), 'feat', BIT_B)]
    slice x0 -> x3, local copies, waits for them, and re-layouts: none -> 9.95 us  [the longest x1 5.61 us: shards(): early_rows = lax.slice_in_dim(tokens, 0, cut)]
  transfers between devices with their start and end apart: 2 -> 9, of which waited for: 0 -> 2; matrix products, arithmetic and copies ran while one was open for 35% -> 2% of each run, Pallas kernels for 0% -> 81%
where the time goes in v1:
time: 466 us
  Pallas kernels  419 us (90%)
  between operations  13.4 us (3%)
  starting transfers between devices  13.2 us (3%)
  local copies, waits for them, and re-layouts  9.97 us (2%)
    pallas_call x6, Pallas kernels, product(): pl.pallas_call(functools.partial(product_kernel, plan), grid=(tiles,), in...  419 us
    ppermute x7, starting transfers between devices, from_partner(): lax.ppermute(array, axis, [(i, i ^ 1 << apart) for i in range(lax.axis_si...  13 us
  transfers between devices with their start and end apart: 9, of which 2 were waited for; matrix products, arithmetic and copies ran while one was open for 2% of the time, Pallas kernels for 81%

profile of v1, /device:TPU:0, one launch (start us, length us, event | category | flops | bytes accessed | tf_op | source)
XLA Modules:
  0.0 466.2 jit_solution(18021524827978623272)
XLA Ops:
  6.5 0.0 copy-start
  6.5 5.6 %slice.10 = bf16[1152,2048]{1,0:T(8,128)(2,1)} slice(bf16[2048,2048]{1,0:T(8,128)(2,1)} %refs_0_), slice={[0:1152], [0:2048]} | slice | bytes 9437184 | tf_op jit(solution)/shard_map/slice | solution.py:170
  12.2 3.0 collective-permute-start
  15.1 2.0 slice.9
  17.2 2.6 collective-permute-start.6
  19.8 0.0 copy-done
  19.8 3.7 fusion
  23.5 0.0 reduce-scatter.2.cloned.1.call-update
  23.5 0.2 all-gather.2.cloned.1.call-start
  23.8 1.0 collective-permute-start.2
  24.8 2.3 slice.11
  27.1 0.3 collective-permute-start.3
  27.4 123.6 %shard_map.46 = (f32[2048,13312]{1,0:T(8,128)}, bf16[384,2048]{1,0:T(8,128)(2,1)}, bf16[512,2048]{1,0:T(8,128)(2,1)}) custom-call(bf16[2048,2048]{1,0:T(8,128)(2,1)} %refs_0_, bf16[3,2048,13312]{2,1,0:T(8,128)(2,1)} %refs_2_.11, bf16[3,2048,13312]{2,1,0:T(8,128)(2,1)} %refs_2_.11), custom_call_target="tpu_custom_call" | custom-call | flops 111669149696 | bytes 171966464 | tf_op jit(solution)/shard_map/pallas_call | solution.py:143
  151.0 0.0 reduce-scatter.2.cloned.1.call-done
  151.0 0.8 collective-permute-done.refs_0_
  151.8 1.8 convert_element_type.9
  153.5 3.1 collective-permute-start.1
  156.7 74.8 %shard_map.47.refs_3_ = f32[2048,13312]{1,0:T(8,128)} custom-call(bf16[1152,2048]{1,0:T(8,128)(2,1)} %collective-permute-done.refs_0_, bf16[3,2048,13312]{2,1,0:T(8,128)(2,1)} %refs_2_.11, bf16[3,2048,13312]{2,1,0:T(8,128)(2,1)} %refs_2_.11, f32[2048,13312]{1,0:T(8,128)} %get-tuple-element.37.refs_3_), custom_call_target="tpu_custom_call", output_to_operand_aliasing={{}: (3, {})} | custom-call | flops 3925868544 | bytes 11370496 | tf_op jit(solution)/shard_map/pallas_call | solution.py:143
  231.5 0.0 collective-permute-done.3.refs_0_
  231.5 0.0 collective-permute-done.2.refs_0_
  231.5 2.5 collective-permute-done.1
  234.0 1.7 add_convert_fusion
  235.7 0.0 all-gather.2.cloned.1.call-update
  235.7 0.1 collective-permute-start.5
  235.8 62.8 %shard_map.48.refs_6_.refs_7_ = f32[2048,13312]{1,0:T(8,128)} custom-call(bf16[896,2048]{1,0:T(8,128)(2,1)} %collective-permute-done.2.refs_0_, bf16[3,2048,13312]{2,1,0:T(8,128)(2,1)} %refs_2_.11, bf16[3,2048,13312]{2,1,0:T(8,128)(2,1)} %refs_2_.11, f32[2048,13312]{1,0:T(8,128)} %shard_map.47.refs_3_), custom_call_target="tpu_custom_call", output_to_operand_aliasing={{}: (3, {})} | custom-call | flops 3053453312 | bytes 9601024 | tf_op jit(solution)/shard_map/pallas_call | solution.py:143
  298.6 2.9 collective-permute-start.4
  301.5 0.0 collective-permute-done.6.refs_0_
  301.5 65.8 %shard_map.49.refs_8_ = bf16[2048,6656]{1,0:T(8,128)(2,1)} custom-call(bf16[896,2048]{1,0:T(8,128)(2,1)} %collective-permute-done.6.refs_0_, bf16[3,2048,13312]{2,1,0:T(8,128)(2,1)} %refs_2_.11, bf16[3,2048,13312]{2,1,0:T(8,128)(2,1)} %refs_2_.11, bf16[2048,256]{1,0:T(8,128)(2,1)} %all-gather.2.cloned.1.call-done.refs_3_.refs_4_, ...), custom_call_target="tpu_custom_call" | custom-call | flops 3435134976 | bytes 7819264 | tf_op jit(solution)/shard_map/pallas_call | solution.py:143
  367.2 0.0 collective-permute-done.5.refs_1_
  367.2 48.8 %shard_map.50.refs_7_ = bf16[2048,6656]{1,0:T(8,128)(2,1)} custom-call(bf16[256,2048]{1,0:T(8,128)(2,1)} %collective-permute-done.3.refs_0_, bf16[384,2048]{1,0:T(8,128)(2,1)} %collective-permute-done.5.refs_1_, bf16[3,2048,13312]{2,1,0:T(8,128)(2,1)} %refs_2_.11, bf16[3,2048,13312]{2,1,0:T(8,128)(2,1)} %refs_2_.11, ...), custom_call_target="tpu_custom_call", output_to_operand_aliasing={{}: (8, {})} | custom-call | flops 39258685440 | bytes 106889216 | tf_op jit(solution)/shard_map/pallas_call | solution.py:143
  416.0 0.0 collective-permute-done.4.refs_0_
  416.0 43.3 %shard_map.51 = bf16[2048,6656]{1,0:T(8,128)(2,1)} custom-call(bf16[512,2048]{1,0:T(8,128)(2,1)} %collective-permute-done.4.refs_0_, bf16[3,2048,13312]{2,1,0:T(8,128)(2,1)} %refs_2_.11, bf16[3,2048,13312]{2,1,0:T(8,128)(2,1)} %refs_2_.11, bf16[2048,256]{1,0:T(8,128)(2,1)} %all-gather.2.cloned.1.call-done.refs_3_.refs_4_, ...), custom_call_target="tpu_custom_call", output_to_operand_aliasing={{}: (7, {})} | custom-call | flops 31406948352 | bytes 97779712 | tf_op jit(solution)/shard_map/pallas_call | solution.py:143
  (8 shorter events, 0.0 us)
Async XLA Ops:
  6.5 13.2 %copy-start = (bf16[2048,256]{1,0:T(8,128)(2,1)S(1)}, bf16[2048,256]{1,0:T(8,128)(2,1)}, u32[]{:S(2)}) copy-start(bf16[2048,256]{1,0:T(8,128)(2,1)} %param.6) | copy-start | bytes 3145732
  6.5 144.5 %reduce-scatter.2.cloned.1.call-start = ((), (), s32[]{:S(2)}) async-start(), calls=%async_computation.1 | async-start | bytes 2621440 | tf_op jit(solution)/shard_map/reduce_scatter | solution.py:181
  6.5 8.6 %copy-start.2 = (bf16[2048,2048]{1,0:T(8,128)(2,1)S(1)}, bf16[2048,2048]{1,0:T(8,128)(2,1)}, u32[]{:S(2)}) copy-start(bf16[2048,2048]{1,0:T(8,128)(2,1)} %refs_0_) | copy-start | bytes 25165828
  12.2 139.6 %collective-permute-start = (bf16[1152,2048]{1,0:T(8,128)(2,1)}, bf16[1152,2048]{1,0:T(8,128)(2,1)}, u32[]{:S(2)}, u32[]{:S(2)}) collective-permute-start(bf16[1152,2048]{1,0:T(8,128)(2,1)} %slice.10), channel_id=1, source_target_pairs={{0,1},{1,0},{2,3},{3,2},{4,5},{5,4},{6,7},{7,6},{8,9},{9,8},{10,11... | collective-permute-start | bytes 14155784 | tf_op jit(solution)/shard_map/ppermute | solution.py:17
  17.2 284.3 %collective-permute-start.6 = (bf16[896,2048]{1,0:T(8,128)(2,1)}, bf16[896,2048]{1,0:T(8,128)(2,1)}, u32[]{:S(2)}, u32[]{:S(2)}) collective-permute-start(bf16[896,2048]{1,0:T(8,128)(2,1)} %slice.9), channel_id=1, source_target_pairs={{0,4},{1,5},{2,6},{3,7},{4,0},{5,1},{6,2},{7,3},{8,12},{9,13},{10,... | collective-permute-start | bytes 11010056 | tf_op jit(solution)/shard_map/ppermute | solution.py:17
  23.5 275.1 %all-gather.2.cloned.1.call-start = ((), (), s32[]{:S(2)}) async-start(), calls=%async_computation.2 | async-start | bytes 1310720 | tf_op jit(solution)/shard_map/all_gather | solution.py:192
  23.8 207.8 %collective-permute-start.2 = (bf16[896,2048]{1,0:T(8,128)(2,1)}, bf16[896,2048]{1,0:T(8,128)(2,1)}, u32[]{:S(2)}, u32[]{:S(2)}) collective-permute-start(bf16[896,2048]{1,0:T(8,128)(2,1)} %slice.9), channel_id=1, source_target_pairs={{0,1},{1,0},{2,3},{3,2},{4,5},{5,4},{6,7},{7,6},{8,9},{9,8},{10,11... | collective-permute-start | bytes 11010056 | tf_op jit(solution)/shard_map/ppermute | solution.py:17
  27.1 204.5 %collective-permute-start.3 = (bf16[256,2048]{1,0:T(8,128)(2,1)}, bf16[256,2048]{1,0:T(8,128)(2,1)}, u32[]{:S(2)}, u32[]{:S(2)}) collective-permute-start(bf16[256,2048]{1,0:T(8,128)(2,1)} %slice.11), channel_id=1, source_target_pairs={{0,4},{1,5},{2,6},{3,7},{4,0},{5,1},{6,2},{7,3},{8,12},{9,13},{10,... | collective-permute-start | bytes 3145736 | tf_op jit(solution)/shard_map/ppermute | solution.py:17
  153.5 80.5 %collective-permute-start.1 = (bf16[512,256]{1,0:T(8,128)(2,1)}, bf16[512,256]{1,0:T(8,128)(2,1)}, u32[]{:S(2)}, u32[]{:S(2)}) collective-permute-start(bf16[512,256]{1,0:T(8,128)(2,1)} %convert_element_type.9), channel_id=1, source_target_pairs={{0,4},{1,5},{2,6},{3,7},{4,0},{5,1},{6,2},{7,3},{8,12},{9,13},{10,... | collective-permute-start | bytes 786440 | tf_op jit(solution)/shard_map/ppermute | solution.py:17
  156.7 77.3 %copy-start.3 = (f32[512,256]{1,0:T(8,128)S(1)}, f32[512,256]{1,0:T(8,128)}, u32[]{:S(2)}) copy-start(f32[512,256]{1,0:T(8,128)} %reduce-scatter.2.cloned.1.call-done) | copy-start | bytes 1572868
  235.7 131.5 %collective-permute-start.5 = (bf16[384,2048]{1,0:T(8,128)(2,1)}, bf16[384,2048]{1,0:T(8,128)(2,1)}, u32[]{:S(2)}, u32[]{:S(2)}) collective-permute-start(bf16[384,2048]{1,0:T(8,128)(2,1)} %get-tuple-element.48), channel_id=1, source_target_pairs={{0,4},{1,5},{2,6},{3,7},{4,0},{5,1},{6,2},{7,3},{8,12},{9,13},{10,... | collective-permute-start | bytes 4718600 | tf_op jit(solution)/shard_map/ppermute | solution.py:17
  298.6 117.5 %collective-permute-start.4 = (bf16[512,2048]{1,0:T(8,128)(2,1)}, bf16[512,2048]{1,0:T(8,128)(2,1)}, u32[]{:S(2)}, u32[]{:S(2)}) collective-permute-start(bf16[512,2048]{1,0:T(8,128)(2,1)} %get-tuple-element.44), channel_id=1, source_target_pairs={{0,4},{1,5},{2,6},{3,7},{4,0},{5,1},{6,2},{7,3},{8,12},{9,13},{10,... | collective-permute-start | bytes 6291464 | tf_op jit(solution)/shard_map/ppermute | solution.py:17
  416.0 43.3 %copy-start.1 = (bf16[2048,256]{1,0:T(8,128)(2,1)S(1)}, bf16[2048,256]{1,0:T(8,128)(2,1)}, u32[]{:S(2)}) copy-start(bf16[2048,256]{1,0:T(8,128)(2,1)} %param.6) | copy-start | bytes 3145732
Sparse Core Ops, SparseCore 0:
  23.6 58.3 reduce-scatter.1
  235.9 27.8 all-gather.1

commit v2 on v1

--- a/solution.py
+++ b/solution.py
@@ -10,7 +10,7 @@
 BIT_A = 0
 BIT_B = 2
 VMEM_LIMIT = 56 * 1024 * 1024
-FIRST_ROWS, HEAD_ROWS, SECOND_ROWS = 9, 2, 5
+FIRST_ROWS, HEAD_ROWS, SECOND_ROWS = 18, 3, 10
 
 
 def from_partner(array, axis, apart):
@@ -163,8 +163,8 @@
 def shards(tile, tokens, block_weights, low_in, low_out):
     rows = tokens.shape[0]
     count = lax.axis_size("feat")
-    cut = rows * FIRST_ROWS // 16
-    head, mid = rows * HEAD_ROWS // 16, rows * SECOND_ROWS // 16
+    cut = rows * FIRST_ROWS // 32
+    head, mid = rows * HEAD_ROWS // 32, rows * SECOND_ROWS // 32
     mix = functools.partial(product, tile, weights=block_weights)
 
     early_rows = lax.slice_in_dim(tokens, 0, cut)
@@ -182,11 +182,11 @@
 
     total, held_a, held_b = mix([([tokens], 0)], sends=[(head, mid - head), (mid, cut - mid)])
     (latent, near_early), total = after((latent, near_early), total)
-    across = from_partner(latent.astype(jnp.bfloat16), "feat", BIT_B)
-
-    total = mix([([near_early], 1)], total=total, cheaper=16)
+    across = from_partner(latent, "feat", BIT_B)
+
+    total = mix([([near_early], 1)], total=total, cheaper=1000)
     (across, near_late, far_head, held_a, held_b), total = after((across, near_late, far_head, held_a, held_b), total)
-    latent = (latent + across.astype(jnp.float32)).astype(jnp.bfloat16)
+    latent = (latent + across).astype(jnp.bfloat16)
     held_a, latent = after(held_a, latent)
     far_a = from_partner(held_a, "feat", BIT_B)
     latent = lax.all_gather(latent, "feat", axis=0, axis_index_groups=sides, tiled=True)
@@ -214,7 +214,7 @@
         rows = tokens.shape[0] // (mesh.shape["groups"] * mesh.shape["dp"])
         half_width = block_weights.shape[2] // 2
         tile = next((t for t in (512, 256, 128) if half_width % t == 0), 0)
-        fits = tile and rows % 256 == 0 and rows <= 2048 and block_weights.shape[1] <= 2048 and block_weights.shape[1] % 128 == 0
+        fits = tile and rows % 512 == 0 and rows <= 2048 and block_weights.shape[1] <= 2048 and block_weights.shape[1] % 128 == 0
         fits = fits and count & (count - 1) == 0 and count > 1 << BIT_B and rows % count == 0 and BIT_A < BIT_B and low_in.shape[1] % 128 == 0
         body = functools.partial(shards, tile) if fits else plain
         return jax.shard_map(body, mesh=mesh, in_specs=in_specs, out_specs=out_specs, check_vma=False)(

time: 466 us -> 466 us (level)
  no operation moved by 1% of the time
where the time goes in v2:
time: 466 us
  Pallas kernels  419 us (90%)
  between operations  13.4 us (3%)
  starting transfers between devices  13.2 us (3%)
  local copies, waits for them, and re-layouts  9.76 us (2%)
  waiting for transfers between devices  5.25 us (1%)
    pallas_call x6, Pallas kernels, product(): pl.pallas_call(functools.partial(product_kernel, plan), grid=(tiles,), in...  419 us
    ppermute x7, starting transfers between devices, from_partner(): lax.ppermute(array, axis, [(i, i ^ 1 << apart) for i in range(lax.axis_si...  13 us
  transfers between devices with their start and end apart: 9, of which 2 were waited for; matrix products, arithmetic and copies ran while one was open for 2% of the time, Pallas kernels for 81%

profile of v2, /device:TPU:0, one launch (start us, length us, event | category | flops | bytes accessed | tf_op | source)
XLA Modules:
  0.0 466.3 jit_solution(2392898865686434593)
XLA Ops:
  6.5 0.0 reduce-scatter.2.cloned.1.call-start
  6.5 5.6 %slice.10 = bf16[1152,2048]{1,0:T(8,128)(2,1)} slice(bf16[2048,2048]{1,0:T(8,128)(2,1)} %refs_0_), slice={[0:1152], [0:2048]} | slice | bytes 9437184 | tf_op jit(solution)/shard_map/slice | solution.py:170
  12.2 3.0 collective-permute-start
  15.1 0.0 copy-done.2
  15.1 2.0 slice.9
  17.2 2.6 collective-permute-start.6
  19.8 3.7 fusion
  23.5 0.0 reduce-scatter.2.cloned.1.call-update
  23.5 0.2 all-gather.2.cloned.1.call-start
  23.8 1.0 collective-permute-start.2
  24.8 2.1 slice.11
  26.8 0.3 collective-permute-start.3
  27.2 123.6 %shard_map.46 = (f32[2048,13312]{1,0:T(8,128)}, bf16[448,2048]{1,0:T(8,128)(2,1)}, bf16[512,2048]{1,0:T(8,128)(2,1)}) custom-call(bf16[2048,2048]{1,0:T(8,128)(2,1)} %refs_0_, bf16[3,2048,13312]{2,1,0:T(8,128)(2,1)} %refs_2_.11, bf16[3,2048,13312]{2,1,0:T(8,128)(2,1)} %refs_2_.11), custom_call_target="tpu_custom_call" | custom-call | flops 111669149696 | bytes 171966464 | tf_op jit(solution)/shard_map/pallas_call | solution.py:143
  150.8 0.0 reduce-scatter.2.cloned.1.call-done
  150.8 0.9 collective-permute-done.refs_0_
  151.8 3.1 collective-permute-start.1
  154.9 74.8 %shard_map.47.refs_3_ = f32[2048,13312]{1,0:T(8,128)} custom-call(bf16[1152,2048]{1,0:T(8,128)(2,1)} %collective-permute-done.refs_0_, bf16[3,2048,13312]{2,1,0:T(8,128)(2,1)} %refs_2_.11, bf16[3,2048,13312]{2,1,0:T(8,128)(2,1)} %refs_2_.11, f32[2048,13312]{1,0:T(8,128)} %get-tuple-element.37.refs_3_), custom_call_target="tpu_custom_call", output_to_operand_aliasing={{}: (3, {})} | custom-call | flops 62813896 | bytes 181927 | tf_op jit(solution)/shard_map/pallas_call | solution.py:143
  229.8 0.0 collective-permute-done.3.refs_0_
  229.8 0.0 collective-permute-done.2.refs_0_
  229.8 4.2 collective-permute-done.1
  234.0 1.8 add_convert_fusion
  235.8 0.0 all-gather.2.cloned.1.call-update
  235.8 0.1 collective-permute-start.5
  235.9 62.8 %shard_map.48.refs_6_.refs_7_ = f32[2048,13312]{1,0:T(8,128)} custom-call(bf16[896,2048]{1,0:T(8,128)(2,1)} %collective-permute-done.2.refs_0_, bf16[3,2048,13312]{2,1,0:T(8,128)(2,1)} %refs_2_.11, bf16[3,2048,13312]{2,1,0:T(8,128)(2,1)} %refs_2_.11, f32[2048,13312]{1,0:T(8,128)} %shard_map.47.refs_3_), custom_call_target="tpu_custom_call", output_to_operand_aliasing={{}: (3, {})} | custom-call | flops 3053453312 | bytes 9601024 | tf_op jit(solution)/shard_map/pallas_call | solution.py:143
  298.7 2.9 collective-permute-start.4
  301.5 0.0 collective-permute-done.6.refs_0_
  301.5 65.8 %shard_map.49.refs_8_ = bf16[2048,6656]{1,0:T(8,128)(2,1)} custom-call(bf16[896,2048]{1,0:T(8,128)(2,1)} %collective-permute-done.6.refs_0_, bf16[3,2048,13312]{2,1,0:T(8,128)(2,1)} %refs_2_.11, bf16[3,2048,13312]{2,1,0:T(8,128)(2,1)} %refs_2_.11, bf16[2048,256]{1,0:T(8,128)(2,1)} %all-gather.2.cloned.1.call-done.refs_3_.refs_4_, ...), custom_call_target="tpu_custom_call" | custom-call | flops 3435134976 | bytes 7819264 | tf_op jit(solution)/shard_map/pallas_call | solution.py:143
  367.3 0.0 collective-permute-done.5.refs_1_
  367.3 48.8 %shard_map.50.refs_7_ = bf16[2048,6656]{1,0:T(8,128)(2,1)} custom-call(bf16[192,2048]{1,0:T(8,128)(2,1)} %collective-permute-done.3.refs_0_, bf16[448,2048]{1,0:T(8,128)(2,1)} %collective-permute-done.5.refs_1_, bf16[3,2048,13312]{2,1,0:T(8,128)(2,1)} %refs_2_.11, bf16[3,2048,13312]{2,1,0:T(8,128)(2,1)} %refs_2_.11, ...), custom_call_target="tpu_custom_call", output_to_operand_aliasing={{}: (8, {})} | custom-call | flops 39258685440 | bytes 106889216 | tf_op jit(solution)/shard_map/pallas_call | solution.py:143
  416.1 0.0 collective-permute-done.4.refs_0_
  416.1 43.3 %shard_map.51 = bf16[2048,6656]{1,0:T(8,128)(2,1)} custom-call(bf16[512,2048]{1,0:T(8,128)(2,1)} %collective-permute-done.4.refs_0_, bf16[3,2048,13312]{2,1,0:T(8,128)(2,1)} %refs_2_.11, bf16[3,2048,13312]{2,1,0:T(8,128)(2,1)} %refs_2_.11, bf16[2048,256]{1,0:T(8,128)(2,1)} %all-gather.2.cloned.1.call-done.refs_3_.refs_4_, ...), custom_call_target="tpu_custom_call", output_to_operand_aliasing={{}: (7, {})} | custom-call | flops 31406948352 | bytes 97779712 | tf_op jit(solution)/shard_map/pallas_call | solution.py:143
  459.4 0.0 copy-done.1
  (7 shorter events, 0.0 us)
Async XLA Ops:
  6.5 13.2 %copy-start = (bf16[2048,256]{1,0:T(8,128)(2,1)S(1)}, bf16[2048,256]{1,0:T(8,128)(2,1)}, u32[]{:S(2)}) copy-start(bf16[2048,256]{1,0:T(8,128)(2,1)} %param.6) | copy-start | bytes 3145732
  6.5 144.3 %reduce-scatter.2.cloned.1.call-start = ((), (), s32[]{:S(2)}) async-start(), calls=%async_computation.1 | async-start | bytes 2621440 | tf_op jit(solution)/shard_map/reduce_scatter | solution.py:181
  6.5 8.6 %copy-start.2 = (bf16[2048,2048]{1,0:T(8,128)(2,1)S(1)}, bf16[2048,2048]{1,0:T(8,128)(2,1)}, u32[]{:S(2)}) copy-start(bf16[2048,2048]{1,0:T(8,128)(2,1)} %refs_0_) | copy-start | bytes 25165828
  12.2 139.6 %collective-permute-start = (bf16[1152,2048]{1,0:T(8,128)(2,1)}, bf16[1152,2048]{1,0:T(8,128)(2,1)}, u32[]{:S(2)}, u32[]{:S(2)}) collective-permute-start(bf16[1152,2048]{1,0:T(8,128)(2,1)} %slice.10), channel_id=1, source_target_pairs={{0,1},{1,0},{2,3},{3,2},{4,5},{5,4},{6,7},{7,6},{8,9},{9,8},{10,11... | collective-permute-start | bytes 14155784 | tf_op jit(solution)/shard_map/ppermute | solution.py:17
  17.2 284.4 %collective-permute-start.6 = (bf16[896,2048]{1,0:T(8,128)(2,1)}, bf16[896,2048]{1,0:T(8,128)(2,1)}, u32[]{:S(2)}, u32[]{:S(2)}) collective-permute-start(bf16[896,2048]{1,0:T(8,128)(2,1)} %slice.9), channel_id=1, source_target_pairs={{0,4},{1,5},{2,6},{3,7},{4,0},{5,1},{6,2},{7,3},{8,12},{9,13},{10,... | collective-permute-start | bytes 11010056 | tf_op jit(solution)/shard_map/ppermute | solution.py:17
  23.5 275.2 %all-gather.2.cloned.1.call-start = ((), (), s32[]{:S(2)}) async-start(), calls=%async_computation.2 | async-start | bytes 1310720 | tf_op jit(solution)/shard_map/all_gather | solution.py:192
  23.8 206.0 %collective-permute-start.2 = (bf16[896,2048]{1,0:T(8,128)(2,1)}, bf16[896,2048]{1,0:T(8,128)(2,1)}, u32[]{:S(2)}, u32[]{:S(2)}) collective-permute-start(bf16[896,2048]{1,0:T(8,128)(2,1)} %slice.9), channel_id=1, source_target_pairs={{0,1},{1,0},{2,3},{3,2},{4,5},{5,4},{6,7},{7,6},{8,9},{9,8},{10,11... | collective-permute-start | bytes 11010056 | tf_op jit(solution)/shard_map/ppermute | solution.py:17
  26.8 202.9 %collective-permute-start.3 = (bf16[192,2048]{1,0:T(8,128)(2,1)}, bf16[192,2048]{1,0:T(8,128)(2,1)}, u32[]{:S(2)}, u32[]{:S(2)}) collective-permute-start(bf16[192,2048]{1,0:T(8,128)(2,1)} %slice.11), channel_id=1, source_target_pairs={{0,4},{1,5},{2,6},{3,7},{4,0},{5,1},{6,2},{7,3},{8,12},{9,13},{10,... | collective-permute-start | bytes 2359304 | tf_op jit(solution)/shard_map/ppermute | solution.py:17
  151.8 82.2 %collective-permute-start.1 = (f32[512,256]{1,0:T(8,128)}, f32[512,256]{1,0:T(8,128)}, u32[]{:S(2)}, u32[]{:S(2)}) collective-permute-start(f32[512,256]{1,0:T(8,128)} %reduce-scatter.2.cloned.1.call-done), channel_id=1, source_target_pairs={{0,4},{1,5},{2,6},{3,7},{4,0},{5,1},{6,2},{7,3},{8,12},{9,13},{10,... | collective-permute-start | bytes 1572872 | tf_op jit(solution)/shard_map/ppermute | solution.py:17
  154.9 79.1 %copy-start.3 = (f32[512,256]{1,0:T(8,128)S(1)}, f32[512,256]{1,0:T(8,128)}, u32[]{:S(2)}) copy-start(f32[512,256]{1,0:T(8,128)} %reduce-scatter.2.cloned.1.call-done) | copy-start | bytes 1572868
  235.8 131.5 %collective-permute-start.5 = (bf16[448,2048]{1,0:T(8,128)(2,1)}, bf16[448,2048]{1,0:T(8,128)(2,1)}, u32[]{:S(2)}, u32[]{:S(2)}) collective-permute-start(bf16[448,2048]{1,0:T(8,128)(2,1)} %get-tuple-element.48), channel_id=1, source_target_pairs={{0,4},{1,5},{2,6},{3,7},{4,0},{5,1},{6,2},{7,3},{8,12},{9,13},{10,... | collective-permute-start | bytes 5505032 | tf_op jit(solution)/shard_map/ppermute | solution.py:17
  298.7 117.5 %collective-permute-start.4 = (bf16[512,2048]{1,0:T(8,128)(2,1)}, bf16[512,2048]{1,0:T(8,128)(2,1)}, u32[]{:S(2)}, u32[]{:S(2)}) collective-permute-start(bf16[512,2048]{1,0:T(8,128)(2,1)} %get-tuple-element.44), channel_id=1, source_target_pairs={{0,4},{1,5},{2,6},{3,7},{4,0},{5,1},{6,2},{7,3},{8,12},{9,13},{10,... | collective-permute-start | bytes 6291464 | tf_op jit(solution)/shard_map/ppermute | solution.py:17
  416.1 43.3 %copy-start.1 = (bf16[2048,256]{1,0:T(8,128)(2,1)S(1)}, bf16[2048,256]{1,0:T(8,128)(2,1)}, u32[]{:S(2)}) copy-start(bf16[2048,256]{1,0:T(8,128)(2,1)} %param.6) | copy-start | bytes 3145732
Sparse Core Ops, SparseCore 0:
  23.6 58.3 reduce-scatter.1
  235.9 27.8 all-gather.1

commit v3 on v2

--- a/solution.py
+++ b/solution.py
@@ -10,7 +10,7 @@
 BIT_A = 0
 BIT_B = 2
 VMEM_LIMIT = 56 * 1024 * 1024
-FIRST_ROWS, HEAD_ROWS, SECOND_ROWS = 18, 3, 10
+FIRST_ROWS, HEAD_ROWS, SECOND_ROWS = 36, 5, 20
 
 
 def from_partner(array, axis, apart):
@@ -163,8 +163,8 @@
 def shards(tile, tokens, block_weights, low_in, low_out):
     rows = tokens.shape[0]
     count = lax.axis_size("feat")
-    cut = rows * FIRST_ROWS // 32
-    head, mid = rows * HEAD_ROWS // 32, rows * SECOND_ROWS // 32
+    cut = rows * FIRST_ROWS // 64
+    head, mid = rows * HEAD_ROWS // 64, rows * SECOND_ROWS // 64
     mix = functools.partial(product, tile, weights=block_weights)
 
     early_rows = lax.slice_in_dim(tokens, 0, cut)
@@ -214,7 +214,7 @@
         rows = tokens.shape[0] // (mesh.shape["groups"] * mesh.shape["dp"])
         half_width = block_weights.shape[2] // 2
         tile = next((t for t in (512, 256, 128) if half_width % t == 0), 0)
-        fits = tile and rows % 512 == 0 and rows <= 2048 and block_weights.shape[1] <= 2048 and block_weights.shape[1] % 128 == 0
+        fits = tile and rows % 1024 == 0 and rows <= 2048 and block_weights.shape[1] <= 2048 and block_weights.shape[1] % 128 == 0
         fits = fits and count & (count - 1) == 0 and count > 1 << BIT_B and rows % count == 0 and BIT_A < BIT_B and low_in.shape[1] % 128 == 0
         body = functools.partial(shards, tile) if fits else plain
         return jax.shard_map(body, mesh=mesh, in_specs=in_specs, out_specs=out_specs, check_vma=False)(

time: 466 us -> 464 us (level)
  no operation moved by 1% of the time
where the time goes in v3:
time: 464 us
  Pallas kernels  419 us (90%)
  between operations  13.5 us (3%)
  starting transfers between devices  13.2 us (3%)
  local copies, waits for them, and re-layouts  9.66 us (2%)
    pallas_call x6, Pallas kernels, product(): pl.pallas_call(functools.partial(product_kernel, plan), grid=(tiles,), in...  419 us
    ppermute x7, starting transfers between devices, from_partner(): lax.ppermute(array, axis, [(i, i ^ 1 << apart) for i in range(lax.axis_si...  13 us
  transfers between devices with their start and end apart: 9, of which 2 were waited for; matrix products, arithmetic and copies ran while one was open for 2% of the time, Pallas kernels for 81%

profile of v3, /device:TPU:0, one launch (start us, length us, event | category | flops | bytes accessed | tf_op | source)
XLA Modules:
  0.0 463.6 jit_solution(3541398236559308175)
XLA Ops:
  6.5 0.0 copy-start
  6.5 0.0 reduce-scatter.2.cloned.1.call-start
  6.5 5.6 %slice.10 = bf16[1152,2048]{1,0:T(8,128)(2,1)} slice(bf16[2048,2048]{1,0:T(8,128)(2,1)} %refs_0_), slice={[0:1152], [0:2048]} | slice | bytes 9437184 | tf_op jit(solution)/shard_map/slice | solution.py:170
  12.2 3.0 collective-permute-start
  15.1 0.0 copy-done.2
  15.1 2.0 slice.9
  17.2 2.6 collective-permute-start.6
  19.8 3.7 fusion
  23.5 0.0 reduce-scatter.2.cloned.1.call-update
  23.5 0.2 all-gather.2.cloned.1.call-start
  23.8 1.0 collective-permute-start.2
  24.8 2.0 slice.11
  26.8 0.3 collective-permute-start.3
  27.1 123.6 %shard_map.46 = (f32[2048,13312]{1,0:T(8,128)}, bf16[480,2048]{1,0:T(8,128)(2,1)}, bf16[512,2048]{1,0:T(8,128)(2,1)}) custom-call(bf16[2048,2048]{1,0:T(8,128)(2,1)} %refs_0_, bf16[3,2048,13312]{2,1,0:T(8,128)(2,1)} %refs_2_.11, bf16[3,2048,13312]{2,1,0:T(8,128)(2,1)} %refs_2_.11), custom_call_target="tpu_custom_call" | custom-call | flops 111669149696 | bytes 171966464 | tf_op jit(solution)/shard_map/pallas_call | solution.py:143
  150.7 0.0 reduce-scatter.2.cloned.1.call-done
  150.7 1.0 collective-permute-done.refs_0_
  151.8 3.1 collective-permute-start.1
  154.9 74.8 %shard_map.47.refs_3_ = f32[2048,13312]{1,0:T(8,128)} custom-call(bf16[1152,2048]{1,0:T(8,128)(2,1)} %collective-permute-done.refs_0_, bf16[3,2048,13312]{2,1,0:T(8,128)(2,1)} %refs_2_.11, bf16[3,2048,13312]{2,1,0:T(8,128)(2,1)} %refs_2_.11, f32[2048,13312]{1,0:T(8,128)} %get-tuple-element.37.refs_3_), custom_call_target="tpu_custom_call", output_to_operand_aliasing={{}: (3, {})} | custom-call | flops 62813896 | bytes 181927 | tf_op jit(solution)/shard_map/pallas_call | solution.py:143
  229.8 0.0 collective-permute-done.3.refs_0_
  229.8 0.0 collective-permute-done.2.refs_0_
  229.8 0.0 collective-permute-done.1
  229.8 1.8 add_convert_fusion
  231.6 2.6 collective-permute-start.5
  234.2 0.0 all-gather.2.cloned.1.call-update
  234.2 62.8 %shard_map.48.refs_6_.refs_7_ = f32[2048,13312]{1,0:T(8,128)} custom-call(bf16[896,2048]{1,0:T(8,128)(2,1)} %collective-permute-done.2.refs_0_, bf16[3,2048,13312]{2,1,0:T(8,128)(2,1)} %refs_2_.11, bf16[3,2048,13312]{2,1,0:T(8,128)(2,1)} %refs_2_.11, f32[2048,13312]{1,0:T(8,128)} %shard_map.47.refs_3_), custom_call_target="tpu_custom_call", output_to_operand_aliasing={{}: (3, {})} | custom-call | flops 3053453312 | bytes 9601024 | tf_op jit(solution)/shard_map/pallas_call | solution.py:143
  297.0 0.3 collective-permute-start.4
  297.3 0.0 collective-permute-done.6.refs_0_
  297.3 65.8 %shard_map.49.refs_8_ = bf16[2048,6656]{1,0:T(8,128)(2,1)} custom-call(bf16[896,2048]{1,0:T(8,128)(2,1)} %collective-permute-done.6.refs_0_, bf16[3,2048,13312]{2,1,0:T(8,128)(2,1)} %refs_2_.11, bf16[3,2048,13312]{2,1,0:T(8,128)(2,1)} %refs_2_.11, bf16[2048,256]{1,0:T(8,128)(2,1)} %all-gather.2.cloned.1.call-done.refs_3_.refs_4_, ...), custom_call_target="tpu_custom_call" | custom-call | flops 3435134976 | bytes 7819264 | tf_op jit(solution)/shard_map/pallas_call | solution.py:143
  363.1 1.7 collective-permute-done.5.refs_1_
  364.8 48.7 %shard_map.50.refs_7_ = bf16[2048,6656]{1,0:T(8,128)(2,1)} custom-call(bf16[160,2048]{1,0:T(8,128)(2,1)} %collective-permute-done.3.refs_0_, bf16[480,2048]{1,0:T(8,128)(2,1)} %collective-permute-done.5.refs_1_, bf16[3,2048,13312]{2,1,0:T(8,128)(2,1)} %refs_2_.11, bf16[3,2048,13312]{2,1,0:T(8,128)(2,1)} %refs_2_.11, ...), custom_call_target="tpu_custom_call", output_to_operand_aliasing={{}: (8, {})} | custom-call | flops 39258685440 | bytes 106889216 | tf_op jit(solution)/shard_map/pallas_call | solution.py:143
  413.5 0.0 collective-permute-done.4.refs_0_
  413.5 43.3 %shard_map.51 = bf16[2048,6656]{1,0:T(8,128)(2,1)} custom-call(bf16[512,2048]{1,0:T(8,128)(2,1)} %collective-permute-done.4.refs_0_, bf16[3,2048,13312]{2,1,0:T(8,128)(2,1)} %refs_2_.11, bf16[3,2048,13312]{2,1,0:T(8,128)(2,1)} %refs_2_.11, bf16[2048,256]{1,0:T(8,128)(2,1)} %all-gather.2.cloned.1.call-done.refs_3_.refs_4_, ...), custom_call_target="tpu_custom_call", output_to_operand_aliasing={{}: (7, {})} | custom-call | flops 31406948352 | bytes 97779712 | tf_op jit(solution)/shard_map/pallas_call | solution.py:143
  (7 shorter events, 0.0 us)
Async XLA Ops:
  6.5 13.2 %copy-start = (bf16[2048,256]{1,0:T(8,128)(2,1)S(1)}, bf16[2048,256]{1,0:T(8,128)(2,1)}, u32[]{:S(2)}) copy-start(bf16[2048,256]{1,0:T(8,128)(2,1)} %param.6) | copy-start | bytes 3145732
  6.5 144.2 %reduce-scatter.2.cloned.1.call-start = ((), (), s32[]{:S(2)}) async-start(), calls=%async_computation.1 | async-start | bytes 2621440 | tf_op jit(solution)/shard_map/reduce_scatter | solution.py:181
  6.5 8.6 %copy-start.2 = (bf16[2048,2048]{1,0:T(8,128)(2,1)S(1)}, bf16[2048,2048]{1,0:T(8,128)(2,1)}, u32[]{:S(2)}) copy-start(bf16[2048,2048]{1,0:T(8,128)(2,1)} %refs_0_) | copy-start | bytes 25165828
  12.2 139.6 %collective-permute-start = (bf16[1152,2048]{1,0:T(8,128)(2,1)}, bf16[1152,2048]{1,0:T(8,128)(2,1)}, u32[]{:S(2)}, u32[]{:S(2)}) collective-permute-start(bf16[1152,2048]{1,0:T(8,128)(2,1)} %slice.10), channel_id=1, source_target_pairs={{0,1},{1,0},{2,3},{3,2},{4,5},{5,4},{6,7},{7,6},{8,9},{9,8},{10,11... | collective-permute-start | bytes 14155784 | tf_op jit(solution)/shard_map/ppermute | solution.py:17
  17.2 280.1 %collective-permute-start.6 = (bf16[896,2048]{1,0:T(8,128)(2,1)}, bf16[896,2048]{1,0:T(8,128)(2,1)}, u32[]{:S(2)}, u32[]{:S(2)}) collective-permute-start(bf16[896,2048]{1,0:T(8,128)(2,1)} %slice.9), channel_id=1, source_target_pairs={{0,4},{1,5},{2,6},{3,7},{4,0},{5,1},{6,2},{7,3},{8,12},{9,13},{10,... | collective-permute-start | bytes 11010056 | tf_op jit(solution)/shard_map/ppermute | solution.py:17
  23.5 273.5 %all-gather.2.cloned.1.call-start = ((), (), s32[]{:S(2)}) async-start(), calls=%async_computation.2 | async-start | bytes 1310720 | tf_op jit(solution)/shard_map/all_gather | solution.py:192
  23.8 206.0 %collective-permute-start.2 = (bf16[896,2048]{1,0:T(8,128)(2,1)}, bf16[896,2048]{1,0:T(8,128)(2,1)}, u32[]{:S(2)}, u32[]{:S(2)}) collective-permute-start(bf16[896,2048]{1,0:T(8,128)(2,1)} %slice.9), channel_id=1, source_target_pairs={{0,1},{1,0},{2,3},{3,2},{4,5},{5,4},{6,7},{7,6},{8,9},{9,8},{10,11... | collective-permute-start | bytes 11010056 | tf_op jit(solution)/shard_map/ppermute | solution.py:17
  26.8 203.0 %collective-permute-start.3 = (bf16[160,2048]{1,0:T(8,128)(2,1)}, bf16[160,2048]{1,0:T(8,128)(2,1)}, u32[]{:S(2)}, u32[]{:S(2)}) collective-permute-start(bf16[160,2048]{1,0:T(8,128)(2,1)} %slice.11), channel_id=1, source_target_pairs={{0,4},{1,5},{2,6},{3,7},{4,0},{5,1},{6,2},{7,3},{8,12},{9,13},{10,... | collective-permute-start | bytes 1966088 | tf_op jit(solution)/shard_map/ppermute | solution.py:17
  151.8 78.0 %collective-permute-start.1 = (f32[512,256]{1,0:T(8,128)}, f32[512,256]{1,0:T(8,128)}, u32[]{:S(2)}, u32[]{:S(2)}) collective-permute-start(f32[512,256]{1,0:T(8,128)} %reduce-scatter.2.cloned.1.call-done), channel_id=1, source_target_pairs={{0,4},{1,5},{2,6},{3,7},{4,0},{5,1},{6,2},{7,3},{8,12},{9,13},{10,... | collective-permute-start | bytes 1572872 | tf_op jit(solution)/shard_map/ppermute | solution.py:17
  154.9 74.9 %copy-start.3 = (f32[512,256]{1,0:T(8,128)S(1)}, f32[512,256]{1,0:T(8,128)}, u32[]{:S(2)}) copy-start(f32[512,256]{1,0:T(8,128)} %reduce-scatter.2.cloned.1.call-done) | copy-start | bytes 1572868
  231.6 133.2 %collective-permute-start.5 = (bf16[480,2048]{1,0:T(8,128)(2,1)}, bf16[480,2048]{1,0:T(8,128)(2,1)}, u32[]{:S(2)}, u32[]{:S(2)}) collective-permute-start(bf16[480,2048]{1,0:T(8,128)(2,1)} %get-tuple-element.48), channel_id=1, source_target_pairs={{0,4},{1,5},{2,6},{3,7},{4,0},{5,1},{6,2},{7,3},{8,12},{9,13},{10,... | collective-permute-start | bytes 5898248 | tf_op jit(solution)/shard_map/ppermute | solution.py:17
  297.0 116.5 %collective-permute-start.4 = (bf16[512,2048]{1,0:T(8,128)(2,1)}, bf16[512,2048]{1,0:T(8,128)(2,1)}, u32[]{:S(2)}, u32[]{:S(2)}) collective-permute-start(bf16[512,2048]{1,0:T(8,128)(2,1)} %get-tuple-element.44), channel_id=1, source_target_pairs={{0,4},{1,5},{2,6},{3,7},{4,0},{5,1},{6,2},{7,3},{8,12},{9,13},{10,... | collective-permute-start | bytes 6291464 | tf_op jit(solution)/shard_map/ppermute | solution.py:17
  413.5 43.3 %copy-start.1 = (bf16[2048,256]{1,0:T(8,128)(2,1)S(1)}, bf16[2048,256]{1,0:T(8,128)(2,1)}, u32[]{:S(2)}) copy-start(bf16[2048,256]{1,0:T(8,128)(2,1)} %param.6) | copy-start | bytes 3145732
Sparse Core Ops, SparseCore 0:
  23.6 58.3 reduce-scatter.1
  234.4 26.2 all-gather.1
